TPU v7x, 32 devices: a whole 2x2x4 slice. The times are simulated.
32 devices in a mesh: dp: 4 (over x, core), ctx: 8 (over z, y).
Axes of the slice: x: 2, y: 2, z: 4, core: 2. Of those that a mesh axis runs over, the one named last changes fastest.
Arguments:
- tokens: bfloat16 [4096, 1536], P(('dp', 'ctx')), may hold values from -6 to 6
- cotangent: bfloat16 [4096, 1536], P(('dp', 'ctx')), may hold values from -6 to 6
- gain_attn: bfloat16 [1536], P(('dp', 'ctx')), may hold values from 0.5 to 1.5
- w_query: bfloat16 [1536, 1536], P(('dp', 'ctx')), may hold values from -0.1875 to 0.1875
- key_weight: bfloat16 [1536, 768], P(('dp', 'ctx')), may hold values from -0.1875 to 0.1875
- value_weight: bfloat16 [1536, 768], P(('dp', 'ctx')), may hold values from -0.15625 to 0.15625
- w_out: bfloat16 [1536, 1536], P(('dp', 'ctx')), may hold values from -2.5 to 2.5
- gain_ffn: bfloat16 [1536], P(('dp', 'ctx')), may hold values from 0.29882812 to 3
- w_gate: bfloat16 [1536, 4096], P(('dp', 'ctx')), may hold values from -0.15625 to 0.15625
- w_up: bfloat16 [1536, 4096], P(('dp', 'ctx')), may hold values from -0.15625 to 0.15625
- w_down: bfloat16 [4096, 1536], P(('dp', 'ctx')), may hold values from -0.1875 to 0.1875
Outputs:
- output: bfloat16 [4096, 1536], P(('dp', 'ctx'))
- grad_tokens: float32 [4096, 1536], P(('dp', 'ctx'))
- grad_gain_attn: float32 [1536], P(('dp', 'ctx'))
- grad_w_query: float32 [1536, 1536], P(('dp', 'ctx'))
- grad_w_key: float32 [1536, 768], P(('dp', 'ctx'))
- grad_w_value: float32 [1536, 768], P(('dp', 'ctx'))
- grad_w_out: float32 [1536, 1536], P(('dp', 'ctx'))
- grad_gain_ffn: float32 [1536], P(('dp', 'ctx'))
- grad_w_gate: float32 [1536, 4096], P(('dp', 'ctx'))
- grad_w_up: float32 [1536, 4096], P(('dp', 'ctx'))
- grad_w_down: float32 [4096, 1536], P(('dp', 'ctx'))
All inputs are finite; a program needn't handle non-finite values.
Results may differ from a plain program's by a relative error of at most 0.028.
Values may be sent and summed in bfloat16 or wider, within the bound.
A program may use at most 320 MiB of HBM per device.

v0:
```python
import functools

import jax
import jax.numpy as jnp
import numpy as np
from jax import lax
from jax.experimental import pallas as pl
from jax.experimental.pallas import tpu as pltpu
from jax.sharding import PartitionSpec as P

QUERY_HEADS = 16
KEY_VALUE_HEADS = 8
HEAD_SIZE = 96


NORM_EPS = 1e-05
ROPE_THETA = 100000.0
MASK_FILL = -1e30


def passed_along(value, axis, by):
    peers = lax.axis_size(axis)
    pairs = [(i, i + by) for i in range(peers) if 0 <= i + by < peers]
    return lax.ppermute(value, axis, pairs)


def shifted(block, axis, distance):
    devices = range(lax.axis_size(axis))
    route = [((i - distance) % len(devices), i) for i in devices]
    return lax.ppermute(block, axis, route)


def rope_tables(first_row, block_count):
    half_dim = HEAD_SIZE // 2
    positions = (first_row + jnp.arange(block_count, dtype=jnp.int32)).astype(jnp.float32)
    frequency = ROPE_THETA ** (-jnp.arange(half_dim, dtype=jnp.float32) * 2.0 / HEAD_SIZE)
    angles = positions[:, None] * frequency[None, :]
    return (jnp.cos(angles)[:, None, :], jnp.sin(angles)[:, None, :])


def apply_rotary(value_rows, cosine_table, sine_values, direction):
    half_dim = HEAD_SIZE // 2
    first_half = value_rows[..., :half_dim]
    second_half = value_rows[..., half_dim:]
    return jnp.concatenate(
        [
            first_half * cosine_table - direction * second_half * sine_values,
            second_half * cosine_table + direction * first_half * sine_values,
        ],
        axis=-1,
    )


def norm_back(grad_normed, inputs, inv_root, gain):
    grad_gain = jnp.sum(grad_normed * inputs * inv_root, axis=0)
    scaled = grad_normed * gain.astype(jnp.float32)
    grad_inputs = inv_root * (
        scaled - inputs * inv_root * inv_root * jnp.mean(scaled * inputs, axis=-1, keepdims=True)
    )
    return (grad_gain, grad_inputs)


def row_product(left, right):
    return jnp.einsum("tc,tf->cf", left, right, preferred_element_type=jnp.float32)


def blockwise_layer(
    tokens,
    cotangent,
    gain_attn,
    w_query,
    key_weight,
    value_weight,
    w_out,
    gain_ffn,
    w_gate,
    w_up,
    w_down,
):
    token_rows = tokens.shape[0]
    head_group = QUERY_HEADS // KEY_VALUE_HEADS
    key_value_width = KEY_VALUE_HEADS * HEAD_SIZE
    query_width = QUERY_HEADS * HEAD_SIZE
    score_scale = HEAD_SIZE ** (-0.5)
    ctx_count = lax.axis_size("ctx")
    ctx_rank = lax.axis_index("ctx")
    first_row = ctx_rank * token_rows
    query_pos = first_row + jnp.arange(token_rows, dtype=jnp.int32)
    attn_full = (
        lax.all_gather(gain_attn, ("dp", "ctx"), axis=0, tiled=True),
        lax.all_gather(w_query, ("dp", "ctx"), axis=0, tiled=True),
        lax.all_gather(key_weight, ("dp", "ctx"), axis=0, tiled=True),
        lax.all_gather(value_weight, ("dp", "ctx"), axis=0, tiled=True),
        lax.all_gather(w_out, ("dp", "ctx"), axis=0, tiled=True),
    )
    gain_one, query_full, key_full, value_full, out_full = attn_full
    inputs = tokens.astype(jnp.float32)
    inv_one = lax.rsqrt(jnp.mean(inputs * inputs, axis=-1, keepdims=True) + NORM_EPS)
    first_normed = (inputs * inv_one * gain_one.astype(jnp.float32)).astype(jnp.bfloat16)
    query_unrotated = jnp.dot(first_normed, query_full, preferred_element_type=jnp.float32).reshape(
        token_rows, QUERY_HEADS, HEAD_SIZE
    )
    key_unrotated = jnp.dot(first_normed, key_full, preferred_element_type=jnp.float32).reshape(
        token_rows, KEY_VALUE_HEADS, HEAD_SIZE
    )
    value_raw = jnp.dot(first_normed, value_full, preferred_element_type=jnp.float32)
    cosine_table, sine_values = rope_tables(first_row, token_rows)
    query_rows = (
        apply_rotary(query_unrotated, cosine_table, sine_values, 1.0)
        .astype(jnp.bfloat16)
        .reshape(token_rows, KEY_VALUE_HEADS, head_group, HEAD_SIZE)
    )
    keys_rot = (
        apply_rotary(key_unrotated, cosine_table, sine_values, 1.0)
        .astype(jnp.bfloat16)
        .reshape(token_rows, key_value_width)
    )
    kv_local = jnp.concatenate([keys_rot, value_raw.astype(jnp.bfloat16)], axis=1)
    starting = (
        jnp.full((KEY_VALUE_HEADS, head_group, token_rows), MASK_FILL, jnp.float32),
        jnp.zeros((KEY_VALUE_HEADS, head_group, token_rows), jnp.float32),
        jnp.zeros((token_rows, KEY_VALUE_HEADS, head_group, HEAD_SIZE), jnp.float32),
    )
    sequence_portion = lax.all_gather(kv_local, "ctx", axis=0, tiled=True)

    def update(state):
        run_max, run_sum, run_acc = state
        block_count = sequence_portion.shape[0]
        key_portion = sequence_portion[:, :key_value_width].reshape(
            block_count, KEY_VALUE_HEADS, HEAD_SIZE
        )
        value_portion = sequence_portion[:, key_value_width:].reshape(
            block_count, KEY_VALUE_HEADS, HEAD_SIZE
        )
        scores = (
            jnp.einsum(
                "tkgd,skd->kgts", query_rows, key_portion, preferred_element_type=jnp.float32
            )
            * score_scale
        )
        key_pos = jnp.arange(block_count, dtype=jnp.int32)
        allowed = key_pos[None, :] <= query_pos[:, None]
        scores = jnp.where(allowed, scores, MASK_FILL)
        new_max = jnp.maximum(run_max, jnp.max(scores, axis=-1))
        expo = jnp.exp(scores - new_max[..., None])
        new_sum = jnp.sum(expo, axis=-1)
        added = jnp.einsum(
            "kgts,skd->tkgd",
            expo.astype(jnp.bfloat16),
            value_portion,
            preferred_element_type=jnp.float32,
        )
        return (new_max, new_sum, added)

    def unchanged(state):
        return state

    run_max, run_sum, run_acc = lax.cond(
        jnp.int32(0) <= first_row + token_rows - 1, update, unchanged, starting
    )
    attn_four = run_acc / jnp.transpose(run_sum, (2, 0, 1))[..., None]
    log_total = run_max + jnp.log(run_sum)
    attn_out = attn_four.reshape(token_rows, query_width)
    attn_low = attn_out.astype(jnp.bfloat16)
    middle = inputs + jnp.dot(attn_low, out_full, preferred_element_type=jnp.float32)
    mlp_full = (
        lax.all_gather(gain_ffn, ("dp", "ctx"), axis=0, tiled=True),
        lax.all_gather(w_gate, ("dp", "ctx"), axis=0, tiled=True),
        lax.all_gather(w_up, ("dp", "ctx"), axis=0, tiled=True),
        lax.all_gather(w_down, ("dp", "ctx"), axis=0, tiled=True),
    )
    gain_two, gate_full, up_full, down_full = mlp_full
    inv_two = lax.rsqrt(jnp.mean(middle * middle, axis=-1, keepdims=True) + NORM_EPS)
    normed_two = (middle * inv_two * gain_two.astype(jnp.float32)).astype(jnp.bfloat16)
    gate_value = jnp.dot(normed_two, gate_full, preferred_element_type=jnp.float32)
    up_value = jnp.dot(normed_two, up_full, preferred_element_type=jnp.float32)
    sigmoid_gate = jax.nn.sigmoid(gate_value)
    silu_gate = gate_value * sigmoid_gate
    hidden = (silu_gate * up_value).astype(jnp.bfloat16)
    output = (middle + jnp.dot(hidden, down_full, preferred_element_type=jnp.float32)).astype(
        jnp.bfloat16
    )
    mlp_back = (
        lax.all_gather(gain_ffn, ("dp", "ctx"), axis=0, tiled=True),
        lax.all_gather(w_gate, ("dp", "ctx"), axis=0, tiled=True),
        lax.all_gather(w_up, ("dp", "ctx"), axis=0, tiled=True),
        lax.all_gather(w_down, ("dp", "ctx"), axis=0, tiled=True),
    )
    gain_two_back, gate_back, up_back, down_back = mlp_back
    grad_out = cotangent.astype(jnp.float32)
    grad_hidden = jnp.einsum("td,fd->tf", cotangent, down_back, preferred_element_type=jnp.float32)
    grad_gate = (
        grad_hidden * up_value * sigmoid_gate * (1.0 + gate_value * (1.0 - sigmoid_gate))
    ).astype(jnp.bfloat16)
    grad_up = (grad_hidden * silu_gate).astype(jnp.bfloat16)
    grad_normed_two = jnp.einsum(
        "tf,cf->tc", grad_gate, gate_back, preferred_element_type=jnp.float32
    ) + jnp.einsum("tf,cf->tc", grad_up, up_back, preferred_element_type=jnp.float32)
    grad_gain_two, grad_middle_norm = norm_back(grad_normed_two, middle, inv_two, gain_two_back)
    grad_middle = grad_out + grad_middle_norm
    gate_up_pair = jnp.concatenate([grad_gate, grad_up], axis=1)
    gate_up_sum = lax.psum_scatter(
        row_product(normed_two, gate_up_pair), ("dp", "ctx"), scatter_dimension=0, tiled=True
    )
    grad_down_sum = lax.psum_scatter(
        row_product(hidden, cotangent), ("dp", "ctx"), scatter_dimension=0, tiled=True
    )
    attn_back = (
        lax.all_gather(gain_attn, ("dp", "ctx"), axis=0, tiled=True),
        lax.all_gather(w_query, ("dp", "ctx"), axis=0, tiled=True),
        lax.all_gather(key_weight, ("dp", "ctx"), axis=0, tiled=True),
        lax.all_gather(value_weight, ("dp", "ctx"), axis=0, tiled=True),
        lax.all_gather(w_out, ("dp", "ctx"), axis=0, tiled=True),
    )
    gain_one_back, query_back, key_back, value_back, out_back = attn_back
    grad_branch = grad_middle.astype(jnp.bfloat16)
    attention_gradient = jnp.einsum(
        "td,cd->tc", grad_branch, out_back, preferred_element_type=jnp.float32
    ).astype(jnp.bfloat16)
    gradient_quad = attention_gradient.reshape(token_rows, KEY_VALUE_HEADS, head_group, HEAD_SIZE)
    delta_rows = jnp.transpose(
        jnp.sum(gradient_quad.astype(jnp.float32) * attn_four, axis=-1), (1, 2, 0)
    )

    def pair_terms(key_value_block, key_first):
        block_count = key_value_block.shape[0]
        key_portion = key_value_block[:, :key_value_width].reshape(
            block_count, KEY_VALUE_HEADS, HEAD_SIZE
        )
        value_portion = key_value_block[:, key_value_width:].reshape(
            block_count, KEY_VALUE_HEADS, HEAD_SIZE
        )
        scores = (
            jnp.einsum(
                "tkgd,skd->kgts", query_rows, key_portion, preferred_element_type=jnp.float32
            )
            * score_scale
        )
        key_pos = key_first + jnp.arange(block_count, dtype=jnp.int32)
        allowed = key_pos[None, :] <= query_pos[:, None]
        scores = jnp.where(allowed, scores, MASK_FILL)
        probs = jnp.exp(scores - log_total[..., None])
        grad_probs = jnp.einsum(
            "tkgd,skd->kgts", gradient_quad, value_portion, preferred_element_type=jnp.float32
        )
        grad_scores = (probs * (grad_probs - delta_rows[..., None])).astype(jnp.bfloat16)
        grad_query = (
            jnp.einsum(
                "kgts,skd->tkgd", grad_scores, key_portion, preferred_element_type=jnp.float32
            )
            * score_scale
        )
        grad_keys = (
            jnp.einsum(
                "kgts,tkgd->skd", grad_scores, query_rows, preferred_element_type=jnp.float32
            )
            * score_scale
        )
        grad_values = jnp.einsum(
            "kgts,tkgd->skd",
            probs.astype(jnp.bfloat16),
            gradient_quad,
            preferred_element_type=jnp.float32,
        )
        return (
            grad_query,
            jnp.concatenate(
                [
                    grad_keys.reshape(block_count, key_value_width),
                    grad_values.reshape(block_count, key_value_width),
                ],
                axis=1,
            ),
        )

    def add_pair(operands):
        kv_use, key_first, grad_query, grad_now = operands
        more_query, more_kv = pair_terms(kv_use, key_first)
        return (grad_query + more_query, grad_now + more_kv)

    def keep_pair(operands):
        return (operands[2], operands[3])

    def cycle_step(step, state):
        kv_now, grad_now, grad_query = state
        owner = (ctx_rank - step + ctx_count) % ctx_count
        kv_next = passed_along(kv_now, "ctx", 1)
        grad_query, grad_now = lax.cond(
            owner <= ctx_rank,
            add_pair,
            keep_pair,
            (kv_now, owner * token_rows, grad_query, grad_now),
        )
        grad_next = shifted(grad_now.astype(jnp.bfloat16), "ctx", 1).astype(grad_now.dtype)
        return (kv_next, grad_next, grad_query)

    cycle_start = (
        kv_local,
        jnp.zeros((token_rows, 2 * key_value_width), jnp.float32),
        jnp.zeros((token_rows, KEY_VALUE_HEADS, head_group, HEAD_SIZE), jnp.float32),
    )
    kv_final, key_value_gradient, grad_query = lax.fori_loop(0, ctx_count, cycle_step, cycle_start)
    grad_query_raw = (
        apply_rotary(
            grad_query.reshape(token_rows, QUERY_HEADS, HEAD_SIZE), cosine_table, sine_values, -1.0
        )
        .reshape(token_rows, query_width)
        .astype(jnp.bfloat16)
    )
    grad_key_raw = (
        apply_rotary(
            key_value_gradient[:, :key_value_width].reshape(token_rows, KEY_VALUE_HEADS, HEAD_SIZE),
            cosine_table,
            sine_values,
            -1.0,
        )
        .reshape(token_rows, key_value_width)
        .astype(jnp.bfloat16)
    )
    grad_value_raw = key_value_gradient[:, key_value_width:].astype(jnp.bfloat16)
    grad_normed_one = (
        jnp.einsum("tq,cq->tc", grad_query_raw, query_back, preferred_element_type=jnp.float32)
        + jnp.einsum("tq,cq->tc", grad_key_raw, key_back, preferred_element_type=jnp.float32)
        + jnp.einsum("tq,cq->tc", grad_value_raw, value_back, preferred_element_type=jnp.float32)
    )
    grad_gain_one, grad_input_norm = norm_back(grad_normed_one, inputs, inv_one, gain_one_back)
    grad_tokens = grad_middle + grad_input_norm
    projection_grads = jnp.concatenate([grad_query_raw, grad_key_raw, grad_value_raw], axis=1)
    qkv_sum = lax.psum_scatter(
        row_product(first_normed, projection_grads), ("dp", "ctx"), scatter_dimension=0, tiled=True
    )
    grad_out_sum = lax.psum_scatter(
        row_product(attn_low, grad_branch), ("dp", "ctx"), scatter_dimension=0, tiled=True
    )
    gain_sums = (
        lax.psum_scatter(grad_gain_one, ("dp", "ctx"), scatter_dimension=0, tiled=True),
        lax.psum_scatter(grad_gain_two, ("dp", "ctx"), scatter_dimension=0, tiled=True),
    )
    ff_width = w_gate.shape[1]
    return (
        output,
        grad_tokens,
        gain_sums[0],
        qkv_sum[:, :query_width],
        qkv_sum[:, query_width : query_width + key_value_width],
        qkv_sum[:, query_width + key_value_width :],
        grad_out_sum,
        gain_sums[1],
        gate_up_sum[:, :ff_width],
        gate_up_sum[:, ff_width:],
        grad_down_sum,
    )


CUBE = 8
BITS = (0, 1, 2)
HEAD_LANES = 128
HALF_LANES = 64
SHARE = 4 * HEAD_LANES
F32 = jnp.float32
BF16 = jnp.bfloat16


class Here:
    def __init__(self):
        dp = lax.axis_index("dp")
        ctx = lax.axis_index("ctx")
        self.core = lax.rem(dp, 2)
        self.far = ctx // 4
        self.own = (dp // 2, lax.rem(ctx // 2, 2), lax.rem(ctx, 2))
        self.shard = self.shard_of(self.own)
        self.at_home = self.own[0] == self.far
        self.sibling = self.device(self.own, core=1 - self.core)
        self.across = self.device(self.own, far=1 - self.far)

    def shard_of(self, bits):
        return bits[0] * 4 + bits[1] * 2 + bits[2]

    def device(self, bits, core=None, far=None):
        core = self.core if core is None else core
        far = self.far if far is None else far
        return (bits[0] * 2 + core, far * 4 + bits[1] * 2 + bits[2])

    def flip(self, *turned, of=None):
        bits = self.own if of is None else of
        return tuple(1 - bit if index in turned else bit for index, bit in enumerate(bits))

    def next(self, bit):
        return self.device(self.flip(bit))

    def others(self):
        return [
            self.flip(*[bit for bit in BITS if code >> (2 - bit) & 1]) for code in range(1, CUBE)
        ]

    def greet(self, partners):
        barrier = pltpu.get_barrier_semaphore()
        for partner in partners:
            pl.semaphore_signal(
                barrier, inc=1, device_id=partner, device_id_type=pl.DeviceIdType.MESH
            )
        pl.semaphore_wait(barrier, len(partners))

    def peers(self):
        return [self.device(bits) for bits in self.others()]

    def same_core(self):
        beyond = [self.device(bits, far=1 - self.far) for bits in self.others() + [self.own]]
        return self.peers() + beyond


def make_send(source, target, sems, device):
    return pltpu.make_async_remote_copy(
        src_ref=source,
        dst_ref=target,
        send_sem=sems[0],
        recv_sem=sems[1],
        device_id=device,
        device_id_type=pl.DeviceIdType.MESH,
    )


def send(*operands):
    copy = make_send(*operands)
    copy.start()
    return copy


class Sems:
    def __init__(self, sent, received):
        self.sent, self.received, self.used = sent, received, 0

    def __call__(self):
        pair = (self.sent.at[self.used], self.received.at[self.used])
        self.used += 1
        return pair


def run_all(*generators):
    live = list(generators)
    while live:
        for one in list(live):
            try:
                next(one)
            except StopIteration:
                live.remove(one)


def play(script, transfers, actions):
    actions = {name: list(some) for name, some in actions.items()}
    for name in script:
        if name in actions:
            actions[name].pop(0)()
        else:
            next(transfers[name], None)
    run_all(*transfers.values())


def in_step(live):
    live = list(live)
    while live:
        for one in list(live):
            try:
                next(one)
            except StopIteration:
                live.remove(one)
        yield


ORDERS = ((0, 1, 2), (1, 2, 0), (2, 0, 1))
ORDERS_Z_FIRST = ((1, 0, 2), (1, 2, 0))


def gather_cube(here, place_of, order, sems, source=None):
    a, b, c = order
    to = lambda bits, bit: send(place_of(bits), place_of(bits), sems(), here.next(bit))
    from_a, from_b = here.flip(a), here.flip(b)
    own = place_of(here.own)
    pairs = [sems() for _ in order]
    first = lambda block: [
        make_send(block, own, pair, here.next(bit)) for pair, bit in zip(pairs, order)
    ]
    a0, b0, c0 = first(own)
    if source is None:
        for copy in (a0, b0, c0):
            copy.start()
    else:

        @pl.when(here.at_home)
        def _():
            for copy in first(source):
                copy.start()

        yield
        yield

        @pl.when(jnp.logical_not(here.at_home))
        def _():
            for copy in (a0, b0, c0):
                copy.start()

    yield
    a0.wait_recv()
    b1, c1 = to(from_a, b), to(from_a, c)
    yield
    b0.wait_recv()
    c2 = to(from_b, c)
    yield
    b1.wait_recv()
    c3 = to(here.flip(a, b), c)
    yield
    for copy in (c0, c1, c2, c3):
        copy.wait_recv()
    for copy in (a0, b0, b1, c0, c1, c2, c3):
        copy.wait_send()


def gather_cube_parts(here, place_of, size, orders, sems, source=None):
    step = size // len(orders)
    live = []
    for index, order in enumerate(orders):
        part = pl.ds(index * step, step)
        live.append(
            gather_cube(
                here,
                functools.partial(place_of, part=part),
                order,
                sems,
                None if source is None else source.at[:, part],
            )
        )
    return in_step(live)


def total_of(*refs):
    total = refs[0][...].astype(F32)
    for ref in refs[1:]:
        total = total + ref[...].astype(F32)
    return total


PAIRS = (((0, 1, 2), (0, 1)), ((1, 2), (0, 2)), ((0,), (2,)), ((1,), ()))


class ReduceStream:
    def __init__(self, here, part_of, slots, out, order, sems):
        self.here, self.part_of, self.slots, self.out = here, part_of, slots, out
        c, b, a = self.order = order
        self.first = [(c, b, a), (c, b), (c, a), (c,)]
        self.copies = [None] * (CUBE - 1)
        self.sems = [sems() for _ in range(CUBE - 1)]
        self.made = set()

    def send(self, turned, slot, bit):
        self.copies[slot] = send(
            self.part_of(self.here.flip(*turned)),
            self.slots(slot),
            self.sems[slot],
            self.here.next(bit),
        )

    def add(self, turned, *slots):
        for slot in slots:
            self.copies[slot].wait_recv()
        spot = self.part_of(self.here.flip(*turned))
        spot[...] = total_of(spot, *[self.slots(slot) for slot in slots]).astype(BF16)

    def after(self, pair):
        c, b, a = self.order
        before = set(self.made)
        self.made |= {frozenset(turned) for turned in PAIRS[pair]}
        for slot, turned in enumerate(self.first):
            if frozenset(turned) in self.made - before:
                self.send(turned, slot, c)
        if self.copies[4] is None and self.copies[0] is not None and frozenset((b, a)) in self.made:
            self.add((b, a), 0)
            self.send((b, a), 4, b)
        if self.copies[5] is None and self.copies[1] is not None and frozenset((b,)) in self.made:
            self.add((b,), 1)
            self.send((b,), 5, b)

    def finish(self):
        _, b, a = self.order
        self.add((a,), 2, 4)
        self.send((a,), 6, a)
        yield
        for slot in (3, 5, 6):
            self.copies[slot].wait_recv()
        self.out[...] = total_of(
            self.part_of(self.here.own), self.slots(3), self.slots(5), self.slots(6)
        )
        yield
        for copy in self.copies:
            copy.wait_send()


def reductions(here, part, slots, out, orders, sems):
    width = out.shape[1] // len(orders)
    return [
        ReduceStream(
            here,
            lambda bits, columns=columns: part.at[here.shard_of(bits), :, columns],
            lambda slot, columns=columns: slots.at[slot, :, columns],
            out.at[:, columns],
            order,
            sems,
        )
        for columns, order in [
            (pl.ds(index * width, width), order) for index, order in enumerate(orders)
        ]
    ]


def swap_home(here, source, target, relay, local_sem, sems, beyond=None):
    beyond = target if beyond is None else beyond
    half = source.shape[1] // 2
    left, right = pl.ds(0, half), pl.ds(half, half)
    there = here.device(here.flip(0), far=1 - here.far)
    local = pltpu.make_async_copy(source, target, local_sem)
    straight = make_send(source.at[:, left], beyond.at[:, left], sems(), there)
    aside = make_send(source.at[:, right], relay, sems(), here.next(0))
    onward = make_send(relay, target.at[:, right], sems(), here.across)

    @pl.when(here.at_home)
    def _():
        local.start()

    @pl.when(jnp.logical_not(here.at_home))
    def _():
        aside.start()
        straight.start()

    yield

    @pl.when(here.at_home)
    def _():
        aside.wait_recv()
        onward.start()

    yield

    @pl.when(here.at_home)
    def _():
        local.wait()

    @pl.when(jnp.logical_not(here.at_home))
    def _():
        straight.wait_recv()
        onward.wait_recv()
        straight.wait_send()
        aside.wait_send()

    yield

    @pl.when(here.at_home)
    def _():
        onward.wait_send()


def spread(here, place_of, sems, ready=()):
    for copy in ready:
        copy.wait()
    over = send(place_of(here.far), place_of(here.far), sems(), here.across)
    beside = send(place_of(here.far), place_of(here.far), sems(), here.sibling)
    yield
    over.wait_recv()
    last = send(place_of(1 - here.far), place_of(1 - here.far), sems(), here.sibling)
    yield
    beside.wait_recv()
    last.wait_recv()
    for copy in (over, beside, last):
        copy.wait_send()


def gather_columns(here, chunks, target, local_sem, sems):
    x, z, y = here.own
    place = target.at[x, here.core, here.far, z, y]
    local = pltpu.make_async_copy(chunks.at[here.shard], place, local_sem)
    local.start()
    copies = [
        send(chunks.at[here.shard_of(bits)], place, sems(), here.device(bits))
        for bits in here.others()
    ]
    yield
    yield from spread(
        here, lambda far: target.at[:, here.core, far], sems, copies + [local]
    )


ANY = pl.BlockSpec(memory_space=pltpu.MemorySpace.HBM)
VMEM = pl.BlockSpec(memory_space=pltpu.MemorySpace.VMEM)
VMEM_BYTES = 62 * 2**20


def params(collective_id):
    return pltpu.CompilerParams(
        collective_id=collective_id, has_side_effects=True, vmem_limit_bytes=VMEM_BYTES
    )


def dma_sems(count):
    return [pltpu.SemaphoreType.DMA((count,)), pltpu.SemaphoreType.DMA((count,))]


def half_blocks(block):
    return pltpu.VMEM((block[0], block[1] // 2), BF16)


QUERY_TILE = 256
SCRIPT = (
    "oxqghxcxcxqxoxcgodocxcocqqx1h11o1g1ocababadbabhabo",
    "PPPPgdgdcchhAAAAGfBfBBBGjGisjiss",
    "Npp2222f3t3t3t3ti4tj4kwktwtNvnvrrrrnrnrnrnvufuijkjwuuu",
)
ORDERS_SPARE_Z = ((1, 0, 2), (1, 2, 0), (0, 1, 2), (2, 1, 0))
ORDERS_Z_LAST = ((0, 2, 1), (2, 0, 1))
ORDERS_ALL = ORDERS + ((0, 2, 1), (1, 0, 2), (2, 1, 0))
FRONT_ORDERS = dict(x=ORDERS_ALL, c=ORDERS_SPARE_Z, o=ORDERS_SPARE_Z, a=ORDERS_ALL)
BACK_ORDERS = dict(r=ORDERS_ALL, t=ORDERS_ALL, s=ORDERS)
NT = (((1,), (1,)), ((), ()))
TN = (((0,), (0,)), ((), ()))


def dot(left, right):
    return jnp.dot(left, right, preferred_element_type=F32)


def dot_nt(left, right):
    return lax.dot_general(left, right, NT, preferred_element_type=F32)


def dot_tn(left, right):
    return lax.dot_general(left, right, TN, preferred_element_type=F32)


def rotate(head, cosine, sine):
    return head * cosine + pltpu.roll(head, HALF_LANES, 1) * sine


def scores_of(keys, queries):
    count = keys.shape[0] - QUERY_TILE
    parts = []
    if count > 0:
        parts.append(dot_nt(keys[:count], queries) * HEAD_SIZE**-0.5)
    last = dot_nt(keys[count:], queries) * HEAD_SIZE**-0.5
    key = lax.broadcasted_iota(jnp.int32, last.shape, 0)
    query = lax.broadcasted_iota(jnp.int32, last.shape, 1)
    parts.append(jnp.where(key <= query, last, MASK_FILL))
    return parts


def attend_tile(q, k, v_t, o_t, ob, lse, group, tile):
    rows = pl.ds(tile * QUERY_TILE, QUERY_TILE)
    count = (tile + 1) * QUERY_TILE
    parts = scores_of(k[:count, :], q[group, rows, :])
    top = jnp.max(parts[-1], axis=0, keepdims=True)
    for part in parts[:-1]:
        top = jnp.maximum(top, jnp.max(part, axis=0, keepdims=True))
    total = jnp.zeros_like(top)
    result = None
    first = 0
    for part in parts:
        expo = jnp.exp(part - top)
        total = total + jnp.sum(expo, axis=0, keepdims=True)
        added = dot(v_t[:, first : first + part.shape[0]], expo.astype(BF16))
        result = added if result is None else result + added
        first += part.shape[0]
    result = result / total
    o_t[group, :, rows] = result
    ob[group * HEAD_SIZE : (group + 1) * HEAD_SIZE, rows] = result[:HEAD_SIZE].astype(BF16)
    lse[group, :, rows] = top + jnp.log(total)


def spaced(head):
    half = HEAD_SIZE // 2
    gap = jnp.zeros((head.shape[0], HALF_LANES - half), head.dtype)
    return jnp.concatenate([head[:, :half], gap, head[:, half:], gap], axis=1)


def packed(head):
    half = HEAD_SIZE // 2
    return jnp.concatenate([head[:, :half], head[:, HALF_LANES : HALF_LANES + half]], axis=1)


def as_column(row):
    size = row.shape[1]
    same = lax.broadcasted_iota(jnp.int32, (size, size), 0) == lax.broadcasted_iota(
        jnp.int32, (size, size), 1
    )
    return jnp.sum(jnp.where(same, row, 0.0), axis=1, keepdims=True)


def cut_projections(w_query, key_weight, value_weight, gain_attn, gain_ffn, chunks):
    query, key, value = (ref[...].astype(F32) for ref in (w_query, key_weight, value_weight))
    rows = query.shape[0]
    gains = [as_column(ref[...].astype(F32)) for ref in (gain_attn, gain_ffn)]
    gap = jnp.zeros((rows, HEAD_LANES - HEAD_SIZE - 2), F32)
    head = lambda weight, index: weight[:, index * HEAD_SIZE : (index + 1) * HEAD_SIZE]
    for shard in range(CUBE):
        parts = [
            spaced(head(query, 2 * shard)),
            spaced(head(query, 2 * shard + 1)),
            spaced(head(key, shard)),
            jnp.concatenate([head(value, shard), *gains, gap], axis=1),
        ]
        chunks[shard] = jnp.concatenate(parts, axis=1).astype(BF16)


def hidden_lanes(shard, part, lanes):
    x, zy = divmod(shard, 4)
    first = (x * 16 + part * 4 + zy) * lanes
    return slice(first, first + lanes)


def chunk_lanes(part, lanes):
    first = (part // 2 * 4 + part % 2) * lanes
    return slice(first, first + lanes), slice(first + 2 * lanes, first + 3 * lanes)


def cut_hidden(w_gate, w_up, chunks, half):
    lanes = chunks.shape[2] // 8
    for shard in range(CUBE):
        for part in (2 * half, 2 * half + 1):
            place = hidden_lanes(shard, part, lanes)
            gate, up = chunk_lanes(part, lanes)
            chunks[shard, :, gate] = w_gate[:, place]
            chunks[shard, :, up] = w_up[:, place]


def norm_after_attention(shards, x_all, ob_all, w_o, gains, y1_own):
    _, block_rows, width = x_all.shape
    rows_of = [
        pl.ds(pl.multiple_of(shard * block_rows, block_rows), block_rows) for shard in shards
    ]
    ob_t = jnp.concatenate([ob_all[:, :, rows].reshape(width, block_rows) for rows in rows_of], axis=1)
    x = jnp.concatenate([x_all[shard] for shard in shards], axis=0)
    y1 = x.astype(F32) + dot_tn(ob_t, w_o[...].reshape(width, width))
    inv_root = lax.rsqrt(jnp.mean(y1 * y1, axis=-1, keepdims=True) + NORM_EPS)
    h2 = (y1 * inv_root * gains[1:2, :]).astype(BF16)
    if y1_own is not None:
        y1_own[...] = y1[block_rows:]
    for index, shard in enumerate(shards):
        x_all[shard] = h2[index * block_rows : (index + 1) * block_rows]


def feed_forward(half, shards, h2_all, ct_all, w_gu, w_d, hidden, d_gu, out_part, dh2_part):
    _, block_rows, width = h2_all.shape
    share = d_gu.shape[1] // 4
    pair = lambda ref: jnp.concatenate([ref[shard] for shard in shards], axis=0)
    rows_of = [
        pl.ds(pl.multiple_of(shard * block_rows, block_rows), block_rows) for shard in shards
    ]
    both = pl.ds(half * 2 * share, 2 * share)
    weight = w_gu[:, :, :, :, :, :, both].reshape(width, 2 * share)
    gate_up = dot(pair(h2_all), weight)
    gate, up = gate_up[:, :share], gate_up[:, share:]
    sig = 1.0 / (1.0 + jnp.exp(-gate))
    silu = gate * sig
    kept = (silu * up).astype(BF16)
    down = w_d[0, half].reshape(share, width)
    d_hidden = dot_nt(pair(ct_all), down)
    d_gate = (d_hidden * up * sig * (1.0 + gate * (1.0 - sig))).astype(BF16)
    d_up = (d_hidden * silu).astype(BF16)
    d_both = jnp.concatenate([d_gate, d_up], axis=1)
    dh2 = dot_nt(d_both, weight)
    out = dot(kept, down)
    for index, (shard, rows) in enumerate(zip(shards, rows_of)):
        block = slice(index * block_rows, (index + 1) * block_rows)
        hidden[rows, pl.ds(half * share, share)] = kept[block]
        d_gu[rows, both] = d_both[block]
        for total, added in ((dh2_part, dh2), (out_part, out)):
            more = added[block]
            if half == 1:
                more = more + total[shard].astype(F32)
            total[shard] = more.astype(BF16)


def attend_back_tile(q, k, k_t, v, do_t, o_t, lse, dk, dv, group, tile):
    rows = pl.ds(tile * QUERY_TILE, QUERY_TILE)
    count = (tile + 1) * QUERY_TILE
    q_rows = q[group, rows, :]
    do_rows = do_t[group * HEAD_SIZE : (group + 1) * HEAD_SIZE, rows]
    do_rows = jnp.concatenate(
        [do_rows, jnp.zeros((HEAD_LANES - HEAD_SIZE, QUERY_TILE), BF16)], axis=0
    )
    delta = jnp.sum(do_rows.astype(F32) * o_t[group, :, rows], axis=0, keepdims=True)
    log_total = lse[group, :, rows]
    dq_t = None
    first = 0
    for part in scores_of(k[:count, :], q_rows):
        keys = slice(first, first + part.shape[0])
        probs = jnp.exp(part - log_total)
        d_probs = dot(v[keys, :], do_rows)
        d_scores = (probs * (d_probs - delta)).astype(BF16)
        dv[keys, :] += dot_nt(probs.astype(BF16), do_rows)
        dk[keys, :] += dot(d_scores, q_rows)
        added = dot(k_t[:, keys], d_scores)
        dq_t = added if dq_t is None else dq_t + added
        first += part.shape[0]
    return jnp.transpose(dq_t) * HEAD_SIZE**-0.5


def add_rows(total, more, piece):
    if len(total.shape) == 5:
        for z in range(2):
            for y in range(2):
                add_rows(total.at[:, z, y], more.at[:, z, y], piece)
        return

    def body(index, carry):
        rows = pl.ds(pl.multiple_of(index * piece, piece), piece)
        for block in range(total.shape[0]):
            total[block, rows, :] = total_of(
                total.at[block, rows, :], more.at[block, rows, :]
            ).astype(BF16)
        return carry

    lax.fori_loop(0, total.shape[1] // piece, body, 0)


def reduce_copies(here, part, beside, over, sems, piece):
    core, far = here.core, here.far
    first = send(part.at[:, 1 - core, 1 - far], beside.at[0], sems(), here.sibling)
    second = send(part.at[:, 1 - core, far], beside.at[1], sems(), here.sibling)
    yield
    first.wait_recv()
    add_rows(part.at[:, core, 1 - far], beside.at[0], piece)
    third = send(part.at[:, core, 1 - far], over, sems(), here.across)
    second.wait_recv()
    add_rows(part.at[:, core, far], beside.at[1], piece)
    yield
    third.wait_recv()
    add_rows(part.at[:, core, far], over, piece)
    for copy in (first, second, third):
        copy.wait_send()


def scatter_columns(here, part, beside, over, out, local_sem, sems):
    rows = out.shape[1]
    yield from reduce_copies(here, part, beside, over, sems, rows)

    def source(bits):
        return part.at[bits[0], here.core, here.far, bits[1], bits[2]]

    local = pltpu.make_async_copy(source(here.own), out.at[here.shard], local_sem)
    local.start()
    copies = [
        send(source(bits), out.at[here.shard], sems(), here.device(bits)) for bits in here.others()
    ]
    yield
    for copy in copies + [local]:
        copy.wait()


def copy_slots(shape):
    rest = (shape[0], *shape[3:])
    return [pltpu.VMEM((2, *rest), BF16), pltpu.VMEM(rest, BF16)]


def norm_back_rows(grad_normed, rows, gain):
    inv_root = lax.rsqrt(jnp.mean(rows * rows, axis=-1, keepdims=True) + NORM_EPS)
    grad_gain, grad_rows = norm_back(grad_normed, rows, inv_root, gain)
    return grad_gain.reshape(1, -1), grad_rows


def sum_everywhere(here, total, slots, sems):
    hops = [here.sibling] + [here.next(bit) for bit in BITS] + [here.across]
    for index, device in enumerate(hops):
        copy = send(total, slots.at[index], sems(), device)
        yield
        copy.wait()
        total[...] += slots[index]


def layer_kernel(
    tokens, cotangent, w_query, key_weight, value_weight, gain_attn, gain_ffn, w_gate, w_up, down, out,
    cosine, sine,
    output_home, grad_home, gu_rows_too, down_sum, qkv_rows, out_rows, gain_out, gu_rows,
    w_qkv, w_gu, w_d, w_o, x_all, ct_all, ob_all, h1, q, k, v, v_t, o_t, lse, gains, x_own, ct_own, y1_own,
    hidden, d_gu, out_part, dh2_part, dh2, slots, x_relay, ct_relay, qkv, gate_up,
    gu_beside, gu_over, gu_beside_too, gu_over_too, down_beside, down_over, qkv_beside, qkv_over,
    wo_part, wo_beside, wo_over, gain_sums, gain_slots, d_middle, pairs, columns, k_t, dk, dv, out_sum,
    own_rows, local, sent, got,
):
    here = Here()
    sems = Sems(sent, got)
    here.greet(here.same_core() + [here.sibling])
    out_slots, dh1_part, dh1, d_qkv = ct_all, x_all, dh2, hidden
    x, z, y = here.own
    width = tokens.shape[1]
    block_rows = tokens.shape[0]
    seq_rows = CUBE * block_rows

    def swapped(source, target, relay, local_sem, orders):
        swap = swap_home(
            here,
            source,
            target.at[here.shard],
            relay,
            local_sem,
            sems,
            target.at[here.shard_of(here.flip(0))],
        )
        gather = gather_cube_parts(
            here,
            lambda bits, part: target.at[here.shard_of(bits), :, part],
            width,
            orders,
            sems,
            source,
        )
        for _ in range(3):
            next(swap)
            next(gather)
            yield
        run_all(swap)
        yield from gather

    def out_gather():
        mine = w_o.at[x, here.core, here.far, z, y]
        kept = pltpu.make_async_copy(out, mine, local.at[3])
        kept.start()
        over = send(out, mine, sems(), here.across)
        yield
        kept.wait()
        over.wait()
        yield from gather_cube_parts(
            here,
            lambda bits, part: w_o.at[bits[0], here.core, :, bits[1], bits[2], :, part],
            width,
            FRONT_ORDERS["o"],
            sems,
        )
        beside = send(w_o.at[:, here.core], w_o.at[:, here.core], sems(), here.sibling)
        yield
        beside.wait()

    def down_gather():
        kept = pltpu.make_async_copy(down, w_d.at[0, here.core, here.far], local.at[2])
        kept.start()
        yield from spread(here, lambda far: w_d.at[0, here.core, far], sems, [kept])

    def qkv_gather():
        cut_projections(w_query, key_weight, value_weight, gain_attn, gain_ffn, qkv)
        yield from gather_columns(here, qkv, w_qkv, local.at[4], sems)

    ff_share = w_gu.shape[6] // 2
    halves = [pl.ds(half * ff_share, ff_share) for half in range(2)]

    def gate_up_gather(half):
        cut_hidden(w_gate, w_up, gate_up, half)
        yield from gather_columns(
            here,
            gate_up.at[:, :, halves[half]],
            w_gu.at[:, :, :, :, :, :, halves[half]],
            local.at[5 + half],
            sems,
        )

    transfers = dict(
        x=swapped(tokens, x_all, x_relay, local.at[0], FRONT_ORDERS["x"]),
        q=qkv_gather(),
        g=gate_up_gather(0),
        h=gate_up_gather(1),
        o=out_gather(),
        d=down_gather(),
        c=swapped(cotangent, ct_all, ct_relay, local.at[1], FRONT_ORDERS["c"]),
    )
    ob = ob_all.at[here.shard]
    turns = [[here.shard_of(here.flip(*bits)) for bits in turned] for turned in PAIRS]

    def norm():
        turned = jnp.transpose(
            w_qkv[:, :, :, :, :, :, 3 * HEAD_LANES :].astype(F32).reshape(width, HEAD_LANES)
        )
        gains[...] = turned[HEAD_SIZE : HEAD_SIZE + 8]
        x_own[...] = x_all[here.shard]

        def norm_block(index, carry):
            rows = x_all[index].astype(F32)
            inv_root = lax.rsqrt(jnp.mean(rows * rows, axis=-1, keepdims=True) + NORM_EPS)
            place = pl.ds(pl.multiple_of(index * block_rows, block_rows), block_rows)
            h1[place, :] = (rows * inv_root * gains[0:1, :]).astype(BF16)
            return carry

        lax.fori_loop(0, CUBE, norm_block, 0)

    def project():
        def project_tile(index, carry):
            rows = pl.ds(pl.multiple_of(index * QUERY_TILE, QUERY_TILE), QUERY_TILE)
            raw = dot(h1[rows, :], w_qkv[...].reshape(width, SHARE))
            cos_rows, sin_rows = cosine[rows, :], sine[rows, :]
            heads = [raw[:, lane : lane + HEAD_LANES] for lane in range(0, SHARE, HEAD_LANES)]
            q[0, rows, :] = rotate(heads[0], cos_rows, sin_rows).astype(BF16)
            q[1, rows, :] = rotate(heads[1], cos_rows, sin_rows).astype(BF16)
            k[rows, :] = rotate(heads[2], cos_rows, sin_rows).astype(BF16)
            v[rows, :] = heads[3].astype(BF16)
            v_t[:, rows] = jnp.transpose(heads[3]).astype(BF16)
            return carry

        lax.fori_loop(0, seq_rows // QUERY_TILE, project_tile, 0)

    def attend(*tiles):
        for tile in tiles:
            for group in range(2):
                attend_tile(q, k, v_t, o_t, ob, lse, group, tile)
        if tiles[-1] % 2 == 1:
            lanes = pl.ds((tiles[-1] - 1) * QUERY_TILE, 2 * QUERY_TILE)
            transfers["ab"[tiles[-1] // 2]] = gather_cube_parts(
                here,
                lambda bits, part: ob_all.at[here.shard_of(bits), part, lanes],
                ob.shape[0],
                FRONT_ORDERS["a"],
                sems,
            )

    def normed_pair(pair):
        own = PAIRS[pair][-1] == ()
        norm_after_attention(turns[pair], x_all, ob_all, w_o, gains, y1_own if own else None)

    bind = functools.partial
    streams = reductions(here, dh2_part, slots, dh2, BACK_ORDERS["s"], sems)

    def feed(half, pair):
        if half == 0 and pair == 0:
            ct_own[...] = ct_all[here.shard]
        feed_forward(
            half, turns[pair], x_all, ct_all, w_gu, w_d, hidden, d_gu, out_part, dh2_part
        )
        if half == 1:
            for stream in streams:
                stream.after(pair)

    def gate_up_grad(half):
        def quarter(index, carry):
            lanes = pl.ds(pl.multiple_of(index * 4 * HEAD_SIZE, 4 * HEAD_SIZE), 4 * HEAD_SIZE)
            left = x_all[:, :, lanes].reshape(seq_rows, 4 * HEAD_SIZE)
            grad = dot_tn(left, d_gu[:, halves[half]]).astype(BF16)
            place = w_gu.at[index // 2, lax.rem(index, 2), :, :, :, :, halves[half]]
            place[...] = grad.reshape(place.shape)
            return carry

        lax.fori_loop(0, 4, quarter, 0)

    def down_grad():
        def quarter(index, carry):
            lanes = pl.ds(pl.multiple_of(index * HEAD_LANES, HEAD_LANES), HEAD_LANES)
            grad = dot_tn(hidden[:, lanes], ct_all[...].reshape(seq_rows, width)).astype(BF16)
            w_d[0, index // 2, lax.rem(index, 2)] = grad
            return carry

        lax.fori_loop(0, 4, quarter, 0)

    weight_rows = out.shape[0]
    share = 2 * HEAD_SIZE

    def gate_up_reduce(half, beside, over, rows):
        yield from scatter_columns(
            here,
            w_gu.at[:, :, :, :, :, :, halves[half]],
            beside,
            over,
            rows,
            local.at[7 + half],
            sems,
        )

    def down_reduce():
        yield from reduce_copies(here, w_d, down_beside, down_over, sems, 32)
        down_sum[...] = w_d[0, here.core, here.far]

    def to_heads():
        rows = pl.ds(pl.multiple_of(here.shard * block_rows, block_rows), block_rows)
        place = columns.at[:, :, rows]
        mine = pltpu.make_async_copy(pairs.at[here.shard], place, local.at[9])
        mine.start()
        copies = [
            send(pairs.at[here.shard_of(bits)], place, sems(), here.device(bits))
            for bits in here.others()
        ]
        yield
        for copy in copies + [mine]:
            copy.wait()

    def reduce_rows(part, slots, out, orders):
        streams = reductions(here, part, slots, out, orders, sems)
        for pair in range(len(PAIRS)):
            for stream in streams:
                stream.after(pair)
            yield
        yield from in_step([stream.finish() for stream in streams])

    def output_reduce():
        yield from reduce_rows(out_part, out_slots, out_sum, BACK_ORDERS["r"])

    def output_swap():
        own_rows[0] = (y1_own[...] + out_sum[...]).astype(BF16)
        yield from swap_home(here, own_rows.at[0], output_home, ct_relay, local.at[12], sems)

    transfers.update(
        f=gate_up_reduce(0, gu_beside, gu_over, gu_rows),
        s=in_step([stream.finish() for stream in streams]),
        i=gate_up_reduce(1, gu_beside_too, gu_over_too, gu_rows_too),
        j=down_reduce(),
        p=to_heads(),
        r=output_reduce(),
        t=reduce_rows(dh1_part, slots, dh1, BACK_ORDERS["t"]),
        k=scatter_columns(here, w_qkv, qkv_beside, qkv_over, qkv_rows, local.at[10], sems),
        w=scatter_columns(here, wo_part, wo_beside, wo_over, out_rows, local.at[11], sems),
        u=output_swap(),
        v=swap_home(here, own_rows.at[1], grad_home, x_relay, local.at[13], sems),
        n=sum_everywhere(here, gain_sums, gain_slots, sems),
    )

    def norm_two():
        grad_gain, grad_rows = norm_back_rows(dh2[...], y1_own[...], gains[1:2, :])
        gain_sums[...] = jnp.zeros_like(gain_sums)
        gain_sums[1:2, :] = grad_gain
        d_middle[...] = ct_own[...].astype(F32) + grad_rows
        da = d_middle[...].astype(BF16)
        pairs[:, 0] = dot_nt(w_o[...].reshape(width, width), da).astype(BF16).reshape(CUBE, share, block_rows)
        pairs[:, 1] = jnp.transpose(d_middle[...]).astype(BF16).reshape(CUBE, share, block_rows)

    def norm_one():
        grad_gain, grad_rows = norm_back_rows(dh1[...], x_own[...].astype(F32), gains[0:1, :])
        gain_sums[0:1, :] = grad_gain
        own_rows[1] = (d_middle[...] + grad_rows).astype(BF16)

    def attention(tile):
        if tile == 0:
            k_t[...] = jnp.transpose(k[...].astype(F32)).astype(BF16)
            dk[...] = jnp.zeros_like(dk)
            dv[...] = jnp.zeros_like(dv)
        rows = pl.ds(tile * QUERY_TILE, QUERY_TILE)
        for group in range(2):
            dq = attend_back_tile(q, k, k_t, v, columns.at[0], o_t, lse, dk, dv, group, tile)
            d_qkv[rows, group * HEAD_LANES : (group + 1) * HEAD_LANES] = rotate(
                dq, cosine[rows, :], -sine[rows, :]
            ).astype(BF16)
        if rows.start + rows.size == seq_rows:
            d_qkv[:, 2 * HEAD_LANES : 3 * HEAD_LANES] = rotate(
                dk[...] * HEAD_SIZE**-0.5, cosine[...], -sine[...]
            ).astype(BF16)
            d_qkv[:, 3 * HEAD_LANES :] = dv[...].astype(BF16)

    def pair_back(pair):
        shards = [here.shard_of(here.flip(*bits)) for bits in PAIRS[pair]]
        some = jnp.concatenate(
            [
                d_qkv[pl.ds(pl.multiple_of(shard * block_rows, block_rows), block_rows), :]
                for shard in shards
            ],
            axis=0,
        )
        rows = dot_nt(some, w_qkv[...].reshape(width, SHARE)).astype(BF16)
        for index, shard in enumerate(shards):
            dh1_part[shard] = rows[index * block_rows : (index + 1) * block_rows]

    def qkv_grad():

        def quarter(index, carry):
            lanes = pl.ds(pl.multiple_of(index * 4 * HEAD_SIZE, 4 * HEAD_SIZE), 4 * HEAD_SIZE)
            grad = dot_tn(h1[:, lanes], d_qkv[...]).astype(BF16)
            w_qkv[index // 2, lax.rem(index, 2)] = grad.reshape(w_qkv.shape[2:])
            return carry

        lax.fori_loop(0, 4, quarter, 0)

    def out_grad():
        for index in range(4):
            left = ob_all[2 * index : 2 * index + 2].reshape(2 * share, seq_rows)
            grad = dot_nt(left, columns[1]).astype(BF16)
            grad = jnp.concatenate(
                [grad, jnp.zeros((2 * share, wo_part.shape[6] - share), BF16)], axis=1
            )
            wo_part[index // 2, index % 2] = grad.reshape(wo_part.shape[2:])

    bind = functools.partial
    everyone = range(len(PAIRS))
    play(
        "".join(SCRIPT),
        transfers,
        {
            "1": [norm, project, bind(attend, 0), bind(attend, 1), bind(attend, 2, 3)],
            "P": [bind(normed_pair, pair) for pair in everyone],
            "A": [bind(feed, 0, pair) for pair in everyone],
            "B": [bind(feed, 1, pair) for pair in everyone],
            "G": [bind(gate_up_grad, 0), down_grad, bind(gate_up_grad, 1)],
            "N": [norm_two, norm_one],
            "2": [bind(attention, tile) for tile in range(seq_rows // QUERY_TILE)],
            "3": [bind(pair_back, pair) for pair in everyone],
            "4": [qkv_grad, out_grad],
        },
    )
    rank = here.device(here.own)
    rank = rank[0] * CUBE + rank[1]
    mine = pltpu.roll(gain_sums[...], lax.rem(width - rank * weight_rows, width), 1)
    gain_out[...] = mine[:, :HEAD_LANES]


def layer(tokens, cotangent, w_query, key_weight, value_weight, gain_attn, gain_ffn, w_gate, w_up, down,
          out, cosine, sine):
    operands = (
        tokens, cotangent, w_query, key_weight, value_weight, gain_attn, gain_ffn, w_gate, w_up, down, out,
        cosine, sine,
    )
    rows, width = tokens.shape
    weight_rows = out.shape[0]
    seq_rows = CUBE * rows
    share = 2 * HEAD_SIZE
    ff_share = 4 * down.shape[0]
    by_row = lambda lanes: (2, 2, 2, 2, 2, weight_rows, lanes)
    low = lambda *dims: pltpu.VMEM(dims, BF16)
    wide = lambda *dims: pltpu.VMEM(dims, F32)
    home = lambda *dims: jax.ShapeDtypeStruct(dims, BF16)
    outs = (
        home(rows, width),
        home(rows, width),
        home(CUBE, weight_rows, ff_share),
        home(*down.shape),
        home(CUBE, weight_rows, SHARE),
        home(CUBE, weight_rows, 2 * HEAD_LANES),
        jax.ShapeDtypeStruct((8, HEAD_LANES), F32),
        home(CUBE, weight_rows, ff_share),
    )
    return pl.pallas_call(
        layer_kernel,
        out_shape=outs,
        in_specs=[VMEM] * len(operands),
        out_specs=(VMEM,) * len(outs),
        scratch_shapes=[
            low(*by_row(SHARE)),
            low(*by_row(2 * ff_share)),
            low(1, 2, 2, *down.shape),
            low(*by_row(width)),
            low(CUBE, rows, width),
            low(CUBE, rows, width),
            low(CUBE, share, seq_rows),
            low(seq_rows, width),
            low(2, seq_rows, HEAD_LANES),
            low(seq_rows, HEAD_LANES),
            low(seq_rows, HEAD_LANES),
            low(HEAD_LANES, seq_rows),
            wide(2, HEAD_LANES, seq_rows),
            wide(2, 1, seq_rows),
            wide(8, width),
            low(rows, width),
            low(rows, width),
            wide(rows, width),
            low(seq_rows, ff_share),
            low(seq_rows, 2 * ff_share),
            low(CUBE, rows, width),
            low(CUBE, rows, width),
            wide(rows, width),
            low(CUBE - 1, rows, width),
            half_blocks(tokens.shape),
            half_blocks(tokens.shape),
            low(CUBE, weight_rows, SHARE),
            low(CUBE, weight_rows, 2 * ff_share),
            *copy_slots(by_row(ff_share)),
            *copy_slots(by_row(ff_share)),
            *copy_slots((1, 2, 2, *down.shape)),
            *copy_slots(by_row(SHARE)),
            low(*by_row(2 * HEAD_LANES)),
            *copy_slots(by_row(2 * HEAD_LANES)),
            wide(8, width),
            wide(5, 8, width),
            wide(rows, width),
            low(CUBE, 2, share, rows),
            low(2, share, seq_rows),
            low(HEAD_LANES, seq_rows),
            wide(seq_rows, HEAD_LANES),
            wide(seq_rows, HEAD_LANES),
            wide(rows, width),
            low(2, rows, width),
            pltpu.SemaphoreType.DMA((14,)),
        ]
        + dma_sems(500),
        compiler_params=params(1),
        name="layer",
    )(*operands)


def finish_kernel(
    output_home, grad_home, gu_rows_too, down_sum, qkv_rows, out_rows, gains, gu_rows,
    output, grad, gate, up, down, query, key, value, out, gain_one, gain_two,
):
    output[...] = output_home[...]
    grad[...] = grad_home[...].astype(F32)
    down[...] = down_sum[...].astype(F32)
    lanes = gu_rows.shape[2] // 4
    for shard in range(CUBE):
        for part in range(4):
            place = hidden_lanes(shard, part, lanes)
            gate_lanes, up_lanes = chunk_lanes(part % 2, lanes)
            rows = (gu_rows, gu_rows_too)[part // 2]
            gate[:, place] = rows[shard, :, gate_lanes].astype(F32)
            up[:, place] = rows[shard, :, up_lanes].astype(F32)
    heads = [
        [
            qkv_rows[shard, :, index * HEAD_LANES : (index + 1) * HEAD_LANES].astype(F32)
            for index in range(4)
        ]
        for shard in range(CUBE)
    ]
    query[...] = jnp.concatenate([packed(head) for some in heads for head in some[:2]], axis=1)
    key[...] = jnp.concatenate([packed(some[2]) for some in heads], axis=1)
    value[...] = jnp.concatenate([some[3][:, :HEAD_SIZE] for some in heads], axis=1)
    out[...] = jnp.concatenate(
        [out_rows[shard, :, : 2 * HEAD_SIZE].astype(F32) for shard in range(CUBE)], axis=1
    )
    gain_one[...] = gains[0, : gain_one.shape[0]]
    gain_two[...] = gains[1, : gain_two.shape[0]]


def finish(parts, ff_width):
    rows, width = parts[0].shape
    weight_rows = parts[2].shape[1]
    out = lambda *dims: jax.ShapeDtypeStruct(dims, F32)
    outs = (
        jax.ShapeDtypeStruct((rows, width), BF16),
        out(rows, width),
        out(weight_rows, ff_width),
        out(weight_rows, ff_width),
        out(*parts[3].shape),
        out(weight_rows, width),
        out(weight_rows, width // 2),
        out(weight_rows, width // 2),
        out(weight_rows, width),
        out(weight_rows),
        out(weight_rows),
    )
    return pl.pallas_call(
        finish_kernel,
        out_shape=outs,
        in_specs=[VMEM] * len(parts),
        out_specs=(VMEM,) * len(outs),
        compiler_params=pltpu.CompilerParams(vmem_limit_bytes=VMEM_BYTES),
        name="finish",
    )(*parts)


def spaced_tables(row_count):
    half = HEAD_SIZE // 2
    frequency = np.float32(ROPE_THETA) ** (-np.arange(half, dtype=np.float32) * 2.0 / HEAD_SIZE)
    angles = np.arange(row_count, dtype=np.float32)[:, None] * frequency.astype(np.float32)[None, :]
    pad = ((0, 0), (0, HALF_LANES - half))
    cosine, sine = np.pad(np.cos(angles), pad), np.pad(np.sin(angles), pad)
    return (
        jnp.asarray(np.concatenate([cosine, cosine], axis=1), F32),
        jnp.asarray(np.concatenate([-sine, sine], axis=1), F32),
    )


def split_layer(
    tokens,
    cotangent,
    gain_attn,
    w_query,
    key_weight,
    value_weight,
    w_out,
    gain_ffn,
    w_gate,
    w_up,
    w_down,
):
    block_rows = tokens.shape[0]
    cosine, sine = spaced_tables(block_rows * CUBE)
    parts = layer(
        tokens, cotangent, w_query, key_weight, value_weight, gain_attn[None], gain_ffn[None], w_gate, w_up,
        w_down, w_out, cosine, sine,
    )
    output, grad, gate, up, down, query, key, value, out, gain_one, gain_two = finish(
        parts, w_gate.shape[1]
    )
    return (output, grad, gain_one, query, key, value, out, gain_two, gate, up, down)


def solution(mesh):
    heads_split = mesh.shape["dp"] == 4 and mesh.shape["ctx"] == KEY_VALUE_HEADS
    return jax.shard_map(
        split_layer if heads_split else blockwise_layer,
        mesh=mesh,
        in_specs=(
            P(("dp", "ctx"), None),
            P(("dp", "ctx"), None),
            P(("dp", "ctx")),
            P(("dp", "ctx"), None),
            P(("dp", "ctx"), None),
            P(("dp", "ctx"), None),
            P(("dp", "ctx"), None),
            P(("dp", "ctx")),
            P(("dp", "ctx"), None),
            P(("dp", "ctx"), None),
            P(("dp", "ctx"), None),
        ),
        out_specs=(
            P(("dp", "ctx"), None),
            P(("dp", "ctx"), None),
            P(("dp", "ctx")),
            P(("dp", "ctx"), None),
            P(("dp", "ctx"), None),
            P(("dp", "ctx"), None),
            P(("dp", "ctx"), None),
            P(("dp", "ctx")),
            P(("dp", "ctx"), None),
            P(("dp", "ctx"), None),
            P(("dp", "ctx"), None),
        ),
        check_vma=False,
    )
```

profile of v0, /device:TPU:0, one launch (start us, length us, event | category | flops | bytes accessed | tf_op | source)
XLA Modules:
  0.0 329.9 jit_solution(2994717809993415521)
XLA Ops:
  0.6 325.1 %layer.1 = (bf16[128,1536]{1,0:T(8,128)(2,1)}, bf16[128,1536]{1,0:T(8,128)(2,1)}, bf16[8,48,512]{2,1,0:T(8,128)(2,1)}, bf16[128,1536]{1,0:T(8,128)(2,1)}, bf16[8...) custom-call(bf16[128,1536]{1,0:T(8,128)(2,1)} %tokens.1, ...), custom_call_target="tpu_custom_call" | custom-call | tf_op jit(solution)/shard_map/layer/pallas_call | solution.py:1326
  325.7 4.0 %finish.1 = (bf16[128,1536]{1,0:T(8,128)(2,1)}, f32[128,1536]{1,0:T(8,128)}, f32[48,4096]{1,0:T(8,128)}, f32[48,4096]{1,0:T(8,128)}, f32[128,1536]{1,0:T(8,128)}...) custom-call(bf16[128,1536]{1,0:T(8,128)(2,1)} %get-tuple-element.30., ...), custom_call_target="tpu_custom_call" | custom-call | tf_op jit(solution)/shard_map/finish/pallas_call | solution.py:1433
where the time goes:
time: 333 us; the launch traced here: 330 us
  Pallas kernels  329 us (99%)
    pallas_call x1, Pallas kernels, layer(): pl.pallas_call(layer_kernel, out_shape=outs, in_specs=[VMEM] * len(operan...  325 us

commit v1 on v0

--- a/solution.py
+++ b/solution.py
@@ -708,9 +708,9 @@
 
 QUERY_TILE = 256
 SCRIPT = (
-    "oxqghxcxcxqxoxcgodocxcocqqx1h11o1g1ocababadbabhabo",
-    "PPPPgdgdcchhAAAAGfBfBBBGjGisjiss",
-    "Npp2222f3t3t3t3ti4tj4kwktwtNvnvrrrrnrnrnrnvufuijkjwuuu",
+    "xqgxhxqxcoxdxqcxogcqxo1c1o1chgo1c1oababadogbabhaboc",
+    "PPPPgdgdhhAAAAGfBfBBBGjGisjiss",
+    "Npp2222f3t3t3t3t4kitj4wktwtrrNvnvrrnrnrrvuijfukwjuuu",
 )
 ORDERS_SPARE_Z = ((1, 0, 2), (1, 2, 0), (0, 1, 2), (2, 1, 0))
 ORDERS_Z_LAST = ((0, 2, 1), (2, 0, 1))
@@ -827,20 +827,21 @@
             chunks[shard, :, up] = w_up[:, place]
 
 
-def norm_after_attention(shards, x_all, ob_all, w_o, gains, y1_own):
+def norm_after_attention(shards, own, x_all, ob_all, w_o, gains, y1_own):
     _, block_rows, width = x_all.shape
-    rows_of = [
-        pl.ds(pl.multiple_of(shard * block_rows, block_rows), block_rows) for shard in shards
-    ]
-    ob_t = jnp.concatenate([ob_all[:, :, rows].reshape(width, block_rows) for rows in rows_of], axis=1)
-    x = jnp.concatenate([x_all[shard] for shard in shards], axis=0)
+    rows = pl.ds(shards[0] * block_rows, len(shards) * block_rows)
+    ob_t = ob_all[:, :, rows].reshape(width, len(shards) * block_rows)
+    x = x_all[pl.ds(shards[0], len(shards))].reshape(len(shards) * block_rows, width)
     y1 = x.astype(F32) + dot_tn(ob_t, w_o[...].reshape(width, width))
     inv_root = lax.rsqrt(jnp.mean(y1 * y1, axis=-1, keepdims=True) + NORM_EPS)
     h2 = (y1 * inv_root * gains[1:2, :]).astype(BF16)
-    if y1_own is not None:
-        y1_own[...] = y1[block_rows:]
     for index, shard in enumerate(shards):
-        x_all[shard] = h2[index * block_rows : (index + 1) * block_rows]
+        block = slice(index * block_rows, (index + 1) * block_rows)
+        x_all[shard] = h2[block]
+
+        @pl.when(own == shard)
+        def _():
+            y1_own[...] = y1[block]
 
 
 def feed_forward(half, shards, h2_all, ct_all, w_gu, w_d, hidden, d_gu, out_part, dh2_part):
@@ -964,12 +965,16 @@
 
 
 def sum_everywhere(here, total, slots, sems):
-    hops = [here.sibling] + [here.next(bit) for bit in BITS] + [here.across]
-    for index, device in enumerate(hops):
-        copy = send(total, slots.at[index], sems(), device)
-        yield
+    peers = here.same_core()
+    copies = [send(total, slots.at[index], sems(), device) for index, device in enumerate(peers)]
+    yield
+    for copy in copies:
         copy.wait()
-        total[...] += slots[index]
+    total[...] += jnp.sum(slots[: len(peers)], axis=0)
+    beside = send(total, slots.at[len(peers)], sems(), here.sibling)
+    yield
+    beside.wait()
+    total[...] += slots[len(peers)]
 
 
 def layer_kernel(
@@ -1115,8 +1120,9 @@
             )
 
     def normed_pair(pair):
-        own = PAIRS[pair][-1] == ()
-        norm_after_attention(turns[pair], x_all, ob_all, w_o, gains, y1_own if own else None)
+        norm_after_attention(
+            (2 * pair, 2 * pair + 1), here.shard, x_all, ob_all, w_o, gains, y1_own
+        )
 
     bind = functools.partial
     streams = reductions(here, dh2_part, slots, dh2, BACK_ORDERS["s"], sems)
@@ -1294,8 +1300,8 @@
     )
     rank = here.device(here.own)
     rank = rank[0] * CUBE + rank[1]
-    mine = pltpu.roll(gain_sums[...], lax.rem(width - rank * weight_rows, width), 1)
-    gain_out[...] = mine[:, :HEAD_LANES]
+    sums = jnp.concatenate([gain_sums[...], jnp.zeros((6, width), F32)], axis=0)
+    gain_out[...] = pltpu.roll(sums, lax.rem(width - rank * weight_rows, width), 1)[:, :HEAD_LANES]
 
 
 def layer(tokens, cotangent, w_query, key_weight, value_weight, gain_attn, gain_ffn, w_gate, w_up, down,
@@ -1363,8 +1369,8 @@
             *copy_slots(by_row(SHARE)),
             low(*by_row(2 * HEAD_LANES)),
             *copy_slots(by_row(2 * HEAD_LANES)),
-            wide(8, width),
-            wide(5, 8, width),
+            wide(2, width),
+            wide(2 * CUBE, 2, width),
             wide(rows, width),
             low(CUBE, 2, share, rows),
             low(2, share, seq_rows),

time: 333 us -> 331 us (level)
    pallas_call x1, Pallas kernels: 325 us -> 322 us  [layer(): pl.pallas_call(layer_kernel, out_shape=outs, in_specs=[VMEM] * len(operan...]
where the time goes in v1:
time: 331 us; the launch traced here: 326 us
  Pallas kernels  326 us (98%)
    pallas_call x1, Pallas kernels, layer(): pl.pallas_call(layer_kernel, out_shape=outs, in_specs=[VMEM] * len(operan...  322 us

profile of v1, /device:TPU:0, one launch (start us, length us, event | category | flops | bytes accessed | tf_op | source)
XLA Modules:
  0.0 326.4 jit_solution(229466967758436254)
XLA Ops:
  0.6 321.5 %layer.1 = (bf16[128,1536]{1,0:T(8,128)(2,1)}, bf16[128,1536]{1,0:T(8,128)(2,1)}, bf16[8,48,512]{2,1,0:T(8,128)(2,1)}, bf16[128,1536]{1,0:T(8,128)(2,1)}, bf16[8...) custom-call(bf16[128,1536]{1,0:T(8,128)(2,1)} %tokens.1, ...), custom_call_target="tpu_custom_call" | custom-call | tf_op jit(solution)/shard_map/layer/pallas_call | solution.py:1332
  322.2 4.0 %finish.1 = (bf16[128,1536]{1,0:T(8,128)(2,1)}, f32[128,1536]{1,0:T(8,128)}, f32[48,4096]{1,0:T(8,128)}, f32[48,4096]{1,0:T(8,128)}, f32[128,1536]{1,0:T(8,128)}...) custom-call(bf16[128,1536]{1,0:T(8,128)(2,1)} %get-tuple-element.30., ...), custom_call_target="tpu_custom_call" | custom-call | tf_op jit(solution)/shard_map/finish/pallas_call | solution.py:1439
